TPU v7x, 32 devices: a whole 2x2x4 slice. The times are simulated.
32 devices in a mesh: dp: 16 (over z, x, core), batch: 2 (over y).
Axes of the slice: x: 2, y: 2, z: 4, core: 2. Of those that a mesh axis runs over, the one named last changes fastest.
Arguments:
- enc_input: bfloat16 [32, 1536, 512], P(('dp', 'batch')), may hold values from -6 to 6
- dec_input: bfloat16 [32, 1024, 512], P(('dp', 'batch')), may hold values from -6 to 6
- patch_counts: int32 [32, 4], P(('dp', 'batch')), may hold values from 1 to 1152, 1440 in all within a row
- table_lengths: int32 [32, 4], P(('dp', 'batch')), may hold values from 1 to 512, 960 in all within a row
- enc_qkv: bfloat16 [3, 512, 384], replicated, may hold values from -0.25 to 0.25
- enc_out_proj: bfloat16 [384, 512], replicated, may hold values from -2.5 to 2.5
- enc_gate_up: bfloat16 [2, 512, 1024], replicated, may hold values from -0.25 to 0.25
- enc_down: bfloat16 [1024, 512], replicated, may hold values from -0.1875 to 0.1875
- enc_gains: bfloat16 [2, 512], replicated, may hold values from 0.099609375 to 1.8984375
- dec_self_qkv: bfloat16 [3, 512, 384], replicated, may hold values from -0.25 to 0.25
- dec_self_out_proj: bfloat16 [384, 512], replicated, may hold values from -2.5 to 2.5
- dec_cross_qkv: bfloat16 [3, 512, 384], replicated, may hold values from -0.25 to 0.25
- dec_cross_out_proj: bfloat16 [384, 512], replicated, may hold values from -2.5 to 2.5
- dec_gate_up: bfloat16 [2, 512, 1024], replicated, may hold values from -0.25 to 0.25
- dec_down: bfloat16 [1024, 512], replicated, may hold values from -0.1875 to 0.1875
- dec_gains: bfloat16 [2, 512], replicated, may hold values from 0.099609375 to 1.8984375
- dec_ffn_gain: bfloat16 [512], replicated, may hold values from 0.099609375 to 1.8984375
- enc_cot: bfloat16 [32, 1536, 512], P(('dp', 'batch')), may hold values from -6 to 6
- dec_cot: bfloat16 [32, 1024, 512], P(('dp', 'batch')), may hold values from -6 to 6
Outputs:
- enc_output: bfloat16 [32, 1536, 512], P(('dp', 'batch'))
- dec_output: bfloat16 [32, 1024, 512], P(('dp', 'batch'))
- enc_input_grad: float32 [32, 1536, 512], P(('dp', 'batch'))
- dec_input_grad: float32 [32, 1024, 512], P(('dp', 'batch'))
- enc_qkv_grad: float32 [3, 512, 384], replicated
- enc_out_proj_grad: float32 [384, 512], replicated
- enc_gate_up_grad: float32 [2, 512, 1024], replicated
- enc_down_grad: float32 [1024, 512], replicated
- enc_gains_grad: float32 [2, 512], replicated
- dec_self_qkv_grad: float32 [3, 512, 384], replicated
- dec_self_out_proj_grad: float32 [384, 512], replicated
- dec_cross_qkv_grad: float32 [3, 512, 384], replicated
- dec_cross_out_proj_grad: float32 [384, 512], replicated
- dec_gate_up_grad: float32 [2, 512, 1024], replicated
- dec_down_grad: float32 [1024, 512], replicated
- dec_gains_grad: float32 [2, 512], replicated
- dec_ffn_gain_grad: float32 [512], replicated
Inputs may be any that keep to these rules, and one draw needn't show every extreme that they name: `patch_counts`: each row's plots take 1536 - 1536 // 16 patch slots in all, in order from the row's start; the slots after them are padding. One plot of every row has exactly 1152 patches. `table_lengths`: each row's tables take 1024 - 1024 // 16 token slots in all, in the order of the plots; the slots after them are padding. One table of every row has exactly 512 tokens.
All inputs are finite; a program needn't handle non-finite values.
Results may differ from a plain program's by a relative error of at most 0.03.
The roundings to bfloat16 on the way count: a program that leaves them out, or rounds other values in their place, can miss the bound.
Values sent between devices are 32-bit elements; how exact they have to be, the bound alone decides.
No kernel may reach another device: no remote copies, remote signals or barrier semaphores. Data moves between devices by JAX's collectives and lax.ppermute only.
A program may use at most 256 MiB of HBM per device.

v0:
```python
import jax
import jax.numpy as jnp
from jax import lax
from jax.sharding import PartitionSpec as P

HEAD_DIM = 64
BLOCK = 512


EPSILON = 1e-06
SCALE = 0.125
NEGATIVE = -1e30


def rms_norm(values, gain_vec):
    return (
        values * lax.rsqrt(jnp.mean(values * values, axis=-1, keepdims=True) + EPSILON) * gain_vec
    )


def norm_backward(values, gain_vec, grad_normed):
    _, pull_back = jax.vjp(rms_norm, values, gain_vec)
    return pull_back(grad_normed)


def gated_gelu(gate_pre, up_pre):
    return jax.nn.gelu(gate_pre, approximate=True) * up_pre


def segment_ids(counts, length):
    ends = jnp.cumsum(counts)
    places = jnp.arange(length, dtype=jnp.int32)
    return jnp.sum((places[:, None] >= ends[None, :]).astype(jnp.int32), axis=1)


def block_scores(query_block, key_heads, seg_block, block_start, key_seg, causal):
    scores = (
        jnp.einsum("qhd,khd->hqk", query_block, key_heads, preferred_element_type=jnp.float32)
        * SCALE
    )
    allowed = seg_block[:, None] == key_seg[None, :]
    if causal:
        query_places = block_start + jnp.arange(seg_block.shape[0], dtype=jnp.int32)
        key_places = jnp.arange(key_seg.shape[0], dtype=jnp.int32)
        allowed = allowed & (query_places[:, None] >= key_places[None, :])
    return jnp.where(allowed[None], scores, NEGATIVE)


def attend_forward(query_rows, key_rows, value_rows, query_seg, key_seg, causal):
    length, row_width = query_rows.shape
    head_count = row_width // HEAD_DIM
    blocks = length // BLOCK
    key_heads = key_rows.reshape(key_rows.shape[0], head_count, HEAD_DIM)
    value_heads = value_rows.reshape(value_rows.shape[0], head_count, HEAD_DIM)
    block_starts = jnp.arange(blocks, dtype=jnp.int32) * BLOCK

    def one_block(block_args):
        query_block, seg_block, block_start = block_args
        scores = block_scores(query_block, key_heads, seg_block, block_start, key_seg, causal)
        row_max = jnp.max(scores, axis=-1, keepdims=True)
        exp_scores = jnp.exp(scores - row_max)
        row_total = jnp.sum(exp_scores, axis=-1, keepdims=True)
        attn_probs = (exp_scores / row_total).astype(jnp.bfloat16)
        attn_mixed = jnp.einsum(
            "hqk,khd->qhd", attn_probs, value_heads, preferred_element_type=jnp.float32
        )
        return (attn_mixed.astype(jnp.bfloat16), row_max[..., 0] + jnp.log(row_total[..., 0]))

    attn_mixed, log_totals = lax.map(
        one_block,
        (
            query_rows.reshape(blocks, BLOCK, head_count, HEAD_DIM),
            query_seg.reshape(blocks, BLOCK),
            block_starts,
        ),
    )
    return (attn_mixed.reshape(length, row_width), log_totals)


def attend_backward(
    query_rows, key_rows, value_rows, log_totals, query_seg, key_seg, causal, grad_mixed
):
    length, row_width = query_rows.shape
    head_count = row_width // HEAD_DIM
    blocks = length // BLOCK
    key_heads = key_rows.reshape(key_rows.shape[0], head_count, HEAD_DIM)
    value_heads = value_rows.reshape(value_rows.shape[0], head_count, HEAD_DIM)
    block_starts = jnp.arange(blocks, dtype=jnp.int32) * BLOCK

    def one_block(carried, block_args):
        key_total, value_total = carried
        query_block, seg_block, block_start, log_block, grad_block = block_args
        scores = block_scores(query_block, key_heads, seg_block, block_start, key_seg, causal)
        attn_probs = jnp.exp(scores - log_block[..., None])
        value_total = value_total + jnp.einsum(
            "hqk,qhd->khd",
            attn_probs.astype(jnp.bfloat16),
            grad_block,
            preferred_element_type=jnp.float32,
        )
        grad_probs = jnp.einsum(
            "qhd,khd->hqk", grad_block, value_heads, preferred_element_type=jnp.float32
        )
        inner_sum = jnp.sum(attn_probs * grad_probs, axis=-1, keepdims=True)
        grad_scores = (attn_probs * (grad_probs - inner_sum)).astype(jnp.bfloat16)
        grad_query = (
            jnp.einsum("hqk,khd->qhd", grad_scores, key_heads, preferred_element_type=jnp.float32)
            * SCALE
        )
        key_total = (
            key_total
            + jnp.einsum(
                "hqk,qhd->khd", grad_scores, query_block, preferred_element_type=jnp.float32
            )
            * SCALE
        )
        return ((key_total, value_total), grad_query.astype(jnp.bfloat16))

    zero_keys = jnp.zeros(key_heads.shape, jnp.float32)
    (key_total, value_total), grad_query = lax.scan(
        one_block,
        (zero_keys, zero_keys),
        (
            query_rows.reshape(blocks, BLOCK, head_count, HEAD_DIM),
            query_seg.reshape(blocks, BLOCK),
            block_starts,
            log_totals,
            grad_mixed.reshape(blocks, BLOCK, head_count, HEAD_DIM),
        ),
    )
    return (
        grad_query.reshape(length, row_width),
        key_total.reshape(-1, row_width).astype(jnp.bfloat16),
        value_total.reshape(-1, row_width).astype(jnp.bfloat16),
    )


def attention_forward(normed, source, qkv_proj, out_proj, query_seg, key_seg, causal):
    query_rows = jnp.dot(normed, qkv_proj[0], preferred_element_type=jnp.float32).astype(
        jnp.bfloat16
    )
    key_rows = jnp.dot(source, qkv_proj[1], preferred_element_type=jnp.float32).astype(jnp.bfloat16)
    value_rows = jnp.dot(source, qkv_proj[2], preferred_element_type=jnp.float32).astype(
        jnp.bfloat16
    )
    attn_mixed, log_totals = attend_forward(
        query_rows, key_rows, value_rows, query_seg, key_seg, causal
    )
    branch = jnp.dot(attn_mixed, out_proj, preferred_element_type=jnp.float32)
    return (branch, (query_rows, key_rows, value_rows, attn_mixed, log_totals))


def attention_backward(
    normed, source, kept_data, qkv_proj, out_proj, query_seg, key_seg, causal, grad_branch
):
    query_rows, key_rows, value_rows, attn_mixed, log_totals = kept_data
    grad_low = grad_branch.astype(jnp.bfloat16)
    grad_out = jnp.dot(attn_mixed.T, grad_low, preferred_element_type=jnp.float32)
    grad_mixed = jnp.dot(grad_low, out_proj.T, preferred_element_type=jnp.float32).astype(
        jnp.bfloat16
    )
    grad_query, grad_key, grad_value = attend_backward(
        query_rows, key_rows, value_rows, log_totals, query_seg, key_seg, causal, grad_mixed
    )
    grad_qkv = jnp.stack(
        [
            jnp.dot(normed.T, grad_query, preferred_element_type=jnp.float32),
            jnp.dot(source.T, grad_key, preferred_element_type=jnp.float32),
            jnp.dot(source.T, grad_value, preferred_element_type=jnp.float32),
        ]
    )
    grad_normed = jnp.dot(grad_query, qkv_proj[0].T, preferred_element_type=jnp.float32)
    grad_source = jnp.dot(grad_key, qkv_proj[1].T, preferred_element_type=jnp.float32) + jnp.dot(
        grad_value, qkv_proj[2].T, preferred_element_type=jnp.float32
    )
    return (grad_qkv, grad_out, grad_normed, grad_source)


def ffn_forward(normed, gate_up, down_proj):
    gate_pre = jnp.dot(normed, gate_up[0], preferred_element_type=jnp.float32)
    up_pre = jnp.dot(normed, gate_up[1], preferred_element_type=jnp.float32)
    hidden = gated_gelu(gate_pre, up_pre).astype(jnp.bfloat16)
    return (
        jnp.dot(hidden, down_proj, preferred_element_type=jnp.float32),
        (gate_pre, up_pre, hidden),
    )


def ffn_backward(normed, kept_data, gate_up, down_proj, grad_branch):
    gate_pre, up_pre, hidden = kept_data
    grad_low = grad_branch.astype(jnp.bfloat16)
    grad_down = jnp.dot(hidden.T, grad_low, preferred_element_type=jnp.float32)
    grad_hidden = jnp.dot(grad_low, down_proj.T, preferred_element_type=jnp.float32)
    _, pull_back = jax.vjp(gated_gelu, gate_pre, up_pre)
    grad_gate, grad_up = pull_back(grad_hidden)
    grad_gate = grad_gate.astype(jnp.bfloat16)
    grad_up = grad_up.astype(jnp.bfloat16)
    grad_pair = jnp.stack(
        [
            jnp.dot(normed.T, grad_gate, preferred_element_type=jnp.float32),
            jnp.dot(normed.T, grad_up, preferred_element_type=jnp.float32),
        ]
    )
    grad_normed = jnp.dot(grad_gate, gate_up[0].T, preferred_element_type=jnp.float32) + jnp.dot(
        grad_up, gate_up[1].T, preferred_element_type=jnp.float32
    )
    return (grad_pair, grad_down, grad_normed)


def encoder_forward(enc_row, enc_seg, scales, weights):
    qkv_proj, out_proj, gate_up, down_proj = weights
    stream_in = enc_row.astype(jnp.float32)
    normed = rms_norm(stream_in, scales[0]).astype(jnp.bfloat16)
    branch, kept_attn = attention_forward(
        normed, normed, qkv_proj, out_proj, enc_seg, enc_seg, False
    )
    middle = stream_in + branch
    normed_ffn = rms_norm(middle, scales[1]).astype(jnp.bfloat16)
    branch_ffn, kept_ffn = ffn_forward(normed_ffn, gate_up, down_proj)
    memory = (middle + branch_ffn).astype(jnp.bfloat16)
    return (memory, (normed, kept_attn, middle, normed_ffn, kept_ffn))


def encoder_backward(enc_row, enc_seg, scales, weights, kept_data, grad_out):
    qkv_proj, out_proj, gate_up, down_proj = weights
    normed, kept_attn, middle, normed_ffn, kept_ffn = kept_data
    grad_pair, grad_down, grad_normed = ffn_backward(
        normed_ffn, kept_ffn, gate_up, down_proj, grad_out
    )
    grad_norm, grad_gain_two = norm_backward(middle, scales[1], grad_normed)
    grad_middle = grad_out + grad_norm
    grad_qkv, grad_proj, grad_normed, grad_source = attention_backward(
        normed, normed, kept_attn, qkv_proj, out_proj, enc_seg, enc_seg, False, grad_middle
    )
    grad_norm, grad_gain_one = norm_backward(
        enc_row.astype(jnp.float32), scales[0], grad_normed + grad_source
    )
    grad_list = (
        grad_qkv,
        grad_proj,
        grad_pair,
        grad_down,
        jnp.stack([grad_gain_one, grad_gain_two]),
    )
    return (grad_middle + grad_norm, grad_list)


def decoder_step(dec_row, memory, enc_seg, dec_seg, scales, weights, grad_out):
    self_qkv, self_proj, cross_qkv, cross_proj, gate_up, down_proj = weights
    stream_in = dec_row.astype(jnp.float32)
    normed_one = rms_norm(stream_in, scales[0]).astype(jnp.bfloat16)
    branch_one, kept_one = attention_forward(
        normed_one, normed_one, self_qkv, self_proj, dec_seg, dec_seg, True
    )
    after_self = stream_in + branch_one
    normed_two = rms_norm(after_self, scales[1]).astype(jnp.bfloat16)
    branch_two, kept_two = attention_forward(
        normed_two, memory, cross_qkv, cross_proj, dec_seg, enc_seg, False
    )
    second = after_self + branch_two
    normed_three = rms_norm(second, scales[2]).astype(jnp.bfloat16)
    branch_three, kept_three = ffn_forward(normed_three, gate_up, down_proj)
    output = (second + branch_three).astype(jnp.bfloat16)
    grad_pair, grad_down, grad_normed = ffn_backward(
        normed_three, kept_three, gate_up, down_proj, grad_out
    )
    grad_norm, grad_gain_three = norm_backward(second, scales[2], grad_normed)
    grad_second = grad_out + grad_norm
    grad_cross, grad_cross_proj, grad_normed, grad_memory = attention_backward(
        normed_two, memory, kept_two, cross_qkv, cross_proj, dec_seg, enc_seg, False, grad_second
    )
    grad_norm, grad_gain_two = norm_backward(after_self, scales[1], grad_normed)
    grad_first = grad_second + grad_norm
    grad_self, grad_self_proj, grad_normed, grad_source = attention_backward(
        normed_one, normed_one, kept_one, self_qkv, self_proj, dec_seg, dec_seg, True, grad_first
    )
    grad_norm, grad_gain_one = norm_backward(stream_in, scales[0], grad_normed + grad_source)
    grad_list = (
        grad_self,
        grad_self_proj,
        grad_cross,
        grad_cross_proj,
        grad_pair,
        grad_down,
        jnp.stack([grad_gain_one, grad_gain_two]),
        grad_gain_three,
    )
    return (output, grad_first + grad_norm, grad_memory, grad_list)


def padded_rows(grad_list):
    flat_grads = jnp.concatenate([member.reshape(-1) for member in grad_list])
    device_count = lax.axis_size(("dp", "batch"))
    row_width = -(-flat_grads.shape[0] // device_count)
    return flat_grads.reshape(device_count, row_width)


def restore(summed_rows, like_list):
    flat_grads = summed_rows.reshape(-1)
    pieces = []
    offset = 0
    for member in like_list:
        pieces.append(flat_grads[offset : offset + member.size].reshape(member.shape))
        offset = offset + member.size
    return tuple(pieces)


def shards(
    enc_input,
    dec_input,
    patch_counts,
    table_lengths,
    enc_qkv,
    enc_out_proj,
    enc_gate_up,
    enc_down,
    enc_gains,
    dec_self_qkv,
    dec_self_out_proj,
    dec_cross_qkv,
    dec_cross_out_proj,
    dec_gate_up,
    dec_down,
    dec_gains,
    dec_ffn_gain,
    enc_cot,
    dec_cot,
):
    enc_weights = (enc_qkv, enc_out_proj, enc_gate_up, enc_down)
    dec_weights = (
        dec_self_qkv,
        dec_self_out_proj,
        dec_cross_qkv,
        dec_cross_out_proj,
        dec_gate_up,
        dec_down,
    )
    enc_scales = enc_gains.astype(jnp.float32)
    dec_pair = dec_gains.astype(jnp.float32)
    dec_scales = (dec_pair[0], dec_pair[1], dec_ffn_gain.astype(jnp.float32))
    enc_length = enc_input.shape[1]
    dec_length = dec_input.shape[1]
    plot_count = patch_counts.shape[1]

    def first_pass(totals, row_data):
        enc_row, dec_row, counts, lengths, cot_row = row_data
        enc_seg = segment_ids(counts, enc_length)
        dec_seg = segment_ids(lengths, dec_length)
        memory, kept_data = encoder_forward(enc_row, enc_seg, enc_scales, enc_weights)
        dec_keep = (dec_seg < plot_count).astype(jnp.float32)[:, None]
        output, grad_dec, grad_memory, grad_list = decoder_step(
            dec_row,
            memory,
            enc_seg,
            dec_seg,
            dec_scales,
            dec_weights,
            cot_row.astype(jnp.float32) * dec_keep,
        )
        new_totals = tuple(
            (total_grad + row_grad for total_grad, row_grad in zip(totals, grad_list))
        )
        return (new_totals, (memory, output, grad_dec, grad_memory, kept_data))

    def second_pass(totals, row_data):
        enc_row, counts, cot_row, grad_memory, kept_data = row_data
        enc_seg = segment_ids(counts, enc_length)
        enc_keep = (enc_seg < plot_count).astype(jnp.float32)[:, None]
        grad_enc, grad_list = encoder_backward(
            enc_row,
            enc_seg,
            enc_scales,
            enc_weights,
            kept_data,
            cot_row.astype(jnp.float32) * enc_keep + grad_memory,
        )
        new_totals = tuple(
            (total_grad + row_grad for total_grad, row_grad in zip(totals, grad_list))
        )
        return (new_totals, grad_enc)

    dec_zero = tuple(
        (jnp.zeros(member.shape, jnp.float32) for member in dec_weights + (dec_gains, dec_ffn_gain))
    )
    enc_zero = tuple(
        (jnp.zeros(member.shape, jnp.float32) for member in enc_weights + (enc_gains,))
    )
    dec_totals, first_rows = lax.scan(
        first_pass, dec_zero, (enc_input, dec_input, patch_counts, table_lengths, dec_cot)
    )
    memories, dec_outputs, dec_grads_in, memory_grads, kept_rows = first_rows
    enc_totals, enc_grads_in = lax.scan(
        second_pass, enc_zero, (enc_input, patch_counts, enc_cot, memory_grads, kept_rows)
    )
    joined = enc_totals + dec_totals
    all_shares = lax.psum_scatter(
        padded_rows(joined), ("dp", "batch"), scatter_dimension=0, tiled=True
    )
    all_final = restore(lax.all_gather(all_shares, ("dp", "batch"), axis=0, tiled=True), joined)
    enc_final = all_final[: len(enc_totals)]
    dec_final = all_final[len(enc_totals) :]
    return (memories, dec_outputs, enc_grads_in, dec_grads_in) + tuple(enc_final) + tuple(dec_final)


def solution(mesh):
    placed = (
        P(("dp", "batch"), None, None),
        P(("dp", "batch"), None, None),
        P(("dp", "batch"), None),
        P(("dp", "batch"), None),
        P(),
        P(),
        P(),
        P(),
        P(),
        P(),
        P(),
        P(),
        P(),
        P(),
        P(),
        P(),
        P(),
        P(("dp", "batch"), None, None),
        P(("dp", "batch"), None, None),
    )
    return jax.shard_map(
        shards,
        mesh=mesh,
        in_specs=placed,
        out_specs=(
            P(("dp", "batch"), None, None),
            P(("dp", "batch"), None, None),
            P(("dp", "batch"), None, None),
            P(("dp", "batch"), None, None),
            P(),
            P(),
            P(),
            P(),
            P(),
            P(),
            P(),
            P(),
            P(),
            P(),
            P(),
            P(),
            P(),
        ),
        check_vma=False,
    )
```

profile of v0, /device:TPU:0, one launch (start us, length us, event | category | flops | bytes accessed | tf_op | source)
XLA Modules:
  0.0 1634.8 jit_solution(9260641957545577160)
XLA Ops:
  28.3 54.3 %while.143 = (s32[]{:T(128)}, bf16[3,512,6,64]{1,3,2,0:T(8,128)(2,1)}, f32[3,6,512]{2,1,0:T(8,128)}, s32[3,512]{1,0:T(4,128)S(1)}, s32[1536]{0:T(1024)S(1)}, /*i...) while((s32[]{:T(128)}, ...), condition=%wide.region_6.7_spmd, body=%wide.region_3.6_spmd.sunk | while | flops 1265562624 | bytes 63030880 | solution.py:69
  120.9 27.9 %while.144 = (s32[]{:T(128)}, bf16[2,512,6,64]{1,3,2,0:T(8,128)(2,1)}, f32[2,6,512]{2,1,0:T(8,128)S(1)}, s32[2,512]{1,0:T(2,128)S(1)}, s32[1024]{0:T(1024)S(1)},...) while((s32[]{:T(128)}, ...), condition=%wide.region_14.15_spmd, body=%wide.region_11.14_spmd.sunk | while | flops 844822016 | bytes 45477016 | solution.py:69
  162.1 34.9 %while.145 = (s32[]{:T(128)}, bf16[2,512,6,64]{1,3,2,0:T(8,128)(2,1)}, f32[2,6,512]{2,1,0:T(8,128)S(1)}, s32[2,512]{1,0:T(2,128)S(1)}, s32[1536]{0:T(1024)S(1)},...) while((s32[]{:T(128)}, ...), condition=%wide.region_19.20_spmd, body=%wide.region_16.19_spmd.sunk | while | flops 1265562624 | bytes 63038564 | solution.py:69
  235.2 126.0 %while.146 = (s32[]{:T(128)}, f32[1536,6,64]{0,2,1:T(8,128)}, f32[1536,6,64]{0,2,1:T(8,128)}, bf16[2,512,6,64]{1,3,2,0:T(8,128)(2,1)}, bf16[2,512,6,64]{1,3,2,0:...) while((s32[]{:T(128)}, f32[1536,6,64]{0,2,1:T(8,128)}, ...), condition=%wide.region_24.25_spmd.clone, body=%wide.region_22.24_spmd.clone.sunk | while | flops 3094803456 | bytes 214803792 | solution.py:120
  245.2 13.8 multiply_reduce_fusion.15
  259.0 17.2 %multiply_convert_fusion.15 = bf16[6,512,1536]{2,1,0:T(8,128)(2,1)} fusion(f32[6,512,1536]{2,1,0:T(8,128)} %get-tuple-element.1502, f32[6,512,1536]{2,1,0:T(8,128)} %fusion.433, f32[6,512]{1,0:T(8,128)S(1)} %get-tuple-element.1503, f32[6,512]{1,0:T(8,128)S(1)} %dynamic-slice_bitcast_fusion.7, pred[512,1536]{1,0:T(8,128)(4,1)S(1)} %broadcast_compare_fusion.10), kind=kLoop, calls=%fused_computation.56.clone.1 | loop fusion | flops 28311552 | bytes 47996928 | tf_op jit(solution)/shard_map/while/body/eval_jaxpr/while/body/eval_jaxpr/convert_element_type | solution.py:105
  307.3 13.8 multiply_reduce_fusion.15
  321.1 17.2 %multiply_convert_fusion.15 = bf16[6,512,1536]{2,1,0:T(8,128)(2,1)} fusion(f32[6,512,1536]{2,1,0:T(8,128)} %get-tuple-element.1502, f32[6,512,1536]{2,1,0:T(8,128)} %fusion.433, f32[6,512]{1,0:T(8,128)S(1)} %get-tuple-element.1503, f32[6,512]{1,0:T(8,128)S(1)} %dynamic-slice_bitcast_fusion.7, pred[512,1536]{1,0:T(8,128)(4,1)S(1)} %broadcast_compare_fusion.10), kind=kLoop, calls=%fused_computation.56.clone.1 | loop fusion | flops 28311552 | bytes 47996928 | tf_op jit(solution)/shard_map/while/body/eval_jaxpr/while/body/eval_jaxpr/convert_element_type | solution.py:105
  383.2 11.5 multiply_convert_fusion.3
  428.9 191.2 %while.147 = (s32[]{:T(128)}, f32[1536,6,64]{0,2,1:T(8,128)}, f32[1536,6,64]{0,2,1:T(8,128)}, bf16[3,512,6,64]{1,3,2,0:T(8,128)(2,1)}, bf16[3,512,6,64]{1,3,2,0:...) while((s32[]{:T(128)}, f32[1536,6,64]{0,2,1:T(8,128)}, ...), condition=%wide.region_28.29_spmd.clone, body=%wide.region_26.28_spmd.clone.sunk | while | flops 3094803456 | bytes 202213072 | solution.py:120
  439.1 14.3 multiply_reduce_fusion.16
  453.5 17.2 %multiply_convert_fusion.16 = bf16[6,512,1536]{2,1,0:T(8,128)(2,1)} fusion(f32[6,512,1536]{2,1,0:T(8,128)} %get-tuple-element.1515, f32[6,512,1536]{2,1,0:T(8,128)} %fusion.446, f32[6,512]{1,0:T(8,128)S(1)} %get-tuple-element.1516, f32[6,512]{1,0:T(8,128)S(1)} %dynamic-slice_bitcast_fusion.8, pred[512,1536]{1,0:T(8,128)(4,1)S(1)} %broadcast_compare_fusion.11), kind=kLoop, calls=%fused_computation.90.clone.1 | loop fusion | flops 28311552 | bytes 47996928 | tf_op jit(solution)/shard_map/while/body/eval_jaxpr/while/body/eval_jaxpr/convert_element_type | solution.py:105
  501.7 14.3 multiply_reduce_fusion.16
  516.1 17.2 %multiply_convert_fusion.16 = bf16[6,512,1536]{2,1,0:T(8,128)(2,1)} fusion(f32[6,512,1536]{2,1,0:T(8,128)} %get-tuple-element.1515, f32[6,512,1536]{2,1,0:T(8,128)} %fusion.446, f32[6,512]{1,0:T(8,128)S(1)} %get-tuple-element.1516, f32[6,512]{1,0:T(8,128)S(1)} %dynamic-slice_bitcast_fusion.8, pred[512,1536]{1,0:T(8,128)(4,1)S(1)} %broadcast_compare_fusion.11), kind=kLoop, calls=%fused_computation.90.clone.1 | loop fusion | flops 28311552 | bytes 47996928 | tf_op jit(solution)/shard_map/while/body/eval_jaxpr/while/body/eval_jaxpr/convert_element_type | solution.py:105
  544.6 11.4 fusion.448
  565.7 14.3 multiply_reduce_fusion.16
  580.1 17.2 %multiply_convert_fusion.16 = bf16[6,512,1536]{2,1,0:T(8,128)(2,1)} fusion(f32[6,512,1536]{2,1,0:T(8,128)} %get-tuple-element.1515, f32[6,512,1536]{2,1,0:T(8,128)} %fusion.446, f32[6,512]{1,0:T(8,128)S(1)} %get-tuple-element.1516, f32[6,512]{1,0:T(8,128)S(1)} %dynamic-slice_bitcast_fusion.8, pred[512,1536]{1,0:T(8,128)(4,1)S(1)} %broadcast_compare_fusion.11), kind=kLoop, calls=%fused_computation.90.clone.1 | loop fusion | flops 28311552 | bytes 47996928 | tf_op jit(solution)/shard_map/while/body/eval_jaxpr/while/body/eval_jaxpr/convert_element_type | solution.py:105
  648.1 67.3 %while.148 = (s32[]{:T(128)}, f32[1024,6,64]{0,2,1:T(8,128)}, f32[1024,6,64]{0,2,1:T(8,128)}, bf16[2,512,6,64]{1,3,2,0:T(8,128)(2,1)}, bf16[2,512,6,64]{1,3,2,0:...) while((s32[]{:T(128)}, f32[1024,6,64]{0,2,1:T(8,128)}, ...), condition=%wide.region_33.34_spmd.clone, body=%wide.region_31.33_spmd.clone.sunk | while | flops 2064381440 | bytes 211001600 | solution.py:120
  783.2 27.1 %reshape.948 = f32[32,172112]{1,0:T(8,128)} reshape(f32[5507584]{0:T(1024)} %constant_dynamic-update-slice_fusion) | data formatting | bytes 44060672 | tf_op jit(solution)/shard_map/reshape | solution.py:295
  810.4 358.8 %all-reduce.3.cloned.1.call-done = f32[32,172112]{1,0:T(8,128)} async-done(((f32[32,172112]{1,0:T(8,128)}), f32[32,172112]{1,0:T(8,128)}) %all-reduce.3.cloned.1.call-update) | async-done | bytes 22030352
  1196.2 115.4 %all-gather.3.cloned.1.call-done = f32[32,1,172112]{2,1,0:T(1,128)} async-done(((f32[1,1,172112]{2,1,0:T(1,128)}), f32[32,1,172112]{2,1,0:T(1,128)}) %all-gather.3.cloned.1.call-update) | async-done | bytes 22030352 | tf_op jit(solution)/shard_map/all_gather | solution.py:399
  1311.6 222.6 %reduce = f32[32,172112]{1,0:T(8,128)} reduce(f32[32,1,172112]{2,1,0:T(1,128)} %all-gather.3.cloned.1.call-done, f32[]{:T(128)} %constant.291), dimensions={1}, to_apply=%all-gather.reduce_sub_computation | reduce | bytes 44060676 | tf_op jit(solution)/shard_map/all_gather | solution.py:399
  1534.2 27.3 %reshape.949 = f32[5507584]{0:T(1024)} reshape(f32[32,172112]{1,0:T(8,128)} %reduce) | data formatting | bytes 44060672 | tf_op jit(solution)/shard_map/reshape | solution.py:299
  1561.5 24.5 %slice.154 = f32[10757,512]{1,0:T(8,128)} reshape(f32[5507584]{0:T(1024)} %reshape.949) | data formatting | bytes 44060672 | tf_op jit(solution)/shard_map/slice | solution.py:303
  (645 shorter events, 661.1 us)
Async XLA Ops:
  7.2 89.4 %copy-start = (bf16[1024,512]{1,0:T(8,128)(2,1)S(1)}, bf16[1024,512]{1,0:T(8,128)(2,1)}, u32[]{:S(2)}) copy-start(bf16[1024,512]{1,0:T(8,128)(2,1)} %param.38) | copy-start | bytes 3145732
  7.2 1162.0 %all-reduce.3.cloned.1.call-start = ((), (), s32[]{:S(2)}) async-start(), calls=%async_computation.1 | async-start | bytes 44072960
  87.0 9.6 copy-start.23
  106.7 45.5 %copy-start.128 = (f32[1,512]{1,0:T(1,128)}, f32[1,512]{1,0:T(1,128)S(1)}, u32[]{:S(2)}) copy-start(f32[1,512]{1,0:T(1,128)S(1)} %get-tuple-element.1130) | copy-start | bytes 6148
  112.0 7.7 copy-start.151
  209.2 16.5 %copy-start.139 = (f32[1024]{0:T(1024)}, f32[1024]{0:T(1024)S(1)}, u32[]{:S(2)}) copy-start(f32[1024]{0:T(1024)S(1)} %compare_convert_fusion.1) | copy-start | bytes 12292
  211.5 8.8 copy-start.81
  235.6 9.6 copy-start.30
  235.6 9.6 copy-start.47
  297.7 9.6 copy-start.30
  297.7 9.6 copy-start.47
  338.3 7.7 copy-start.4
  338.3 7.7 copy-start.71
  383.2 11.6 copy-start.45
  383.2 11.6 copy-start.93
  429.3 9.8 copy-start.29
  492.0 9.7 copy-start.29
  533.2 7.6 copy-start.5
  556.0 9.7 copy-start.29
  597.2 7.6 copy-start.5
  664.3 11.6 copy-start.3
  696.9 12.1 copy-start.3
  810.3 362.9 %copy-start.125 = (f32[1024]{0:T(1024)S(1)}, f32[1024]{0:T(1024)}, u32[]{:S(2)}) copy-start(f32[1024]{0:T(1024)} %copy-done.124) | copy-start | bytes 12292
  810.4 501.2 %all-gather.3.cloned.1.call-start = ((), (), s32[]{:S(2)}) async-start(), calls=%async_computation | async-start | bytes 22725120 | tf_op jit(solution)/shard_map/all_gather | solution.py:399
  (155 other events, 461.4 us)
Sparse Core Ops, SparseCore 0:
  810.5 358.6 all-reduce.2
  1173.3 138.1 all-gather.2
where the time goes:
time: 1650 us; the launch traced here: 1630 us
  matrix products  491 us (30%)
  waiting for transfers between devices  474 us (29%)
  other arithmetic  386 us (23%)
  local copies, waits for them, and re-layouts  265 us (16%)
    unnamed x3, waiting for transfers between devices  359 us
    all_gather x1, other arithmetic, shards(): lax.all_gather(all_shares, ('dp', 'batch'), axis=0, tiled=True)  223 us
    all_gather x1, waiting for transfers between devices, shards(): lax.all_gather(all_shares, ('dp', 'batch'), axis=0, tiled=True)  115 us
    convert_element_type x7, other arithmetic, one_block(): grad_scores = (attn_probs * (grad_probs - inner_sum)).astype(jnp.bfloat16)  96 us
    dot_general x7, matrix products, one_block(): jnp.einsum('qhd,khd->hqk', grad_block, value_heads, preferred_element_typ...  83.2 us
    unnamed x341, local copies, waits for them, and re-layouts  80.3 us
    dot_general x14, matrix products, block_scores(): jnp.einsum('qhd,khd->hqk', query_block, key_heads, preferred_element_type...  76.7 us
    dot_general x7, matrix products, one_block(): jnp.einsum('hqk,qhd->khd', attn_probs.astype(jnp.bfloat16), grad_block, p...  66.1 us
  transfers between devices with their start and end apart: 2, of which 2 were waited for; matrix products, arithmetic and copies ran while one was open for 1% of the time, Pallas kernels for 0%

commit v1 on v0

v1 whole, which is shorter than its diff:
```python
import functools

import jax
import jax.numpy as jnp
from jax import lax
from jax.experimental import pallas as pl
from jax.experimental.pallas import tpu as pltpu
from jax.sharding import PartitionSpec as P

BF = jnp.bfloat16
F32 = jnp.float32
EPS = 1e-06
NEG = -1e30
SCALE = 0.125
PLAIN = (((1,), (0,)), ((), ()))
NT = (((1,), (1,)), ((), ()))
TN = (((0,), (0,)), ((), ()))
AXES = ("dp", "batch")
GELU_C = 0.7978845608028654
GELU_A = 0.044715


def dot(a, b, dims=PLAIN):
    return lax.dot_general(a, b, dims, preferred_element_type=F32)


def bounds(counts):
    ends, total = [], 0
    for p in range(counts.shape[1]):
        total = total + counts[0, p]
        ends.append(total)
    return ends


def big_plot(counts, ends, size):
    index, start = jnp.int32(0), jnp.int32(0)
    for p in range(1, counts.shape[1]):
        hit = counts[0, p] == size
        index = jnp.where(hit, p, index)
        start = jnp.where(hit, ends[p - 1], start)
    return index, start


def segments(rotated, start, ends, length):
    slot = rotated + start
    slot = jnp.where(slot >= length, slot - length, slot)
    seg = jnp.zeros(rotated.shape, jnp.int32)
    for end in ends:
        seg = seg + (slot >= end).astype(jnp.int32)
    return seg


def iota(shape, dim):
    return lax.broadcasted_iota(jnp.int32, shape, dim)


def wrap(offset, length):
    return jnp.where(offset >= length, offset - length, offset)


def inverse_rms(x):
    return lax.rsqrt(jnp.mean(x * x, axis=1, keepdims=True) + EPS)


def norm_back(x, gain, grad):
    s = inverse_rms(x)
    xs = x * s
    gg = grad * gain
    inner = jnp.mean(gg * xs, axis=1, keepdims=True)
    return s * (gg - xs * inner), jnp.sum(grad * xs, axis=0, keepdims=True)


def fill_rotation(ring, source, length, extra, step=128):
    for r in range(0, length, step):
        ring[r : r + step, :] = source[r : r + step, :].astype(F32)
    ring[length : length + extra, :] = ring[0:extra, :]


def rotated_rows(ring, offset, count):
    base = pl.multiple_of((offset // 8) * 8, 8)
    sub = offset - base
    block = ring[pl.ds(base, count + 8), :]
    shape = (count // 8, 8, block.shape[1])
    turn = lax.rem(8 - sub, 8)
    first = pltpu.roll(block[0:count].reshape(shape), turn, 1)
    second = pltpu.roll(block[8 : count + 8].reshape(shape), turn, 1)
    return jnp.where(iota(shape, 1) < 8 - sub, first, second).reshape(count, shape[2])


def lanes_low(rows):
    return iota((rows, 128), 1) < 64


def head_of(x, low, h):
    zero = jnp.zeros_like(x)
    return jnp.where(low, x, zero) if h == 0 else jnp.where(low, zero, x)


def with_ones(v, low, h):
    one = jnp.ones_like(v)
    return jnp.where(low, v, one) if h == 0 else jnp.where(low, one, v)


def scores_of(qh, parts, sl):
    out = []
    for k, _, lo, hi, bias in parts:
        s = dot(qh, k[lo:hi, sl], NT)
        if bias is not None:
            s = s + bias()
        out.append(s)
    return out


def attend(q, rows, parts, mixed, lse, pairs):
    r0, r1 = rows
    low = lanes_low(r1 - r0)
    for pair in range(pairs):
        sl = slice(pair * 128, pair * 128 + 128)
        qp = q[r0:r1, sl]
        accs, tops = [], []
        for h in range(2):
            all_s = scores_of(head_of(qp, low, h), parts, sl)
            top = jnp.max(all_s[0], axis=1, keepdims=True)
            for s in all_s[1:]:
                top = jnp.maximum(top, jnp.max(s, axis=1, keepdims=True))
            acc = None
            for s, (_, v, lo, hi, _) in zip(all_s, parts):
                p = jnp.exp(s - top).astype(BF)
                term = dot(p, with_ones(v[lo:hi, sl], lanes_low(hi - lo), h))
                acc = term if acc is None else acc + term
            accs.append(acc)
            tops.append(top)
        total = pltpu.roll(jnp.where(low, accs[1], accs[0]), 64, 1)
        mixed[r0:r1, sl] = (jnp.where(low, accs[0], accs[1]) / total).astype(BF)
        lse[r0:r1, sl] = jnp.where(low, tops[0], tops[1]) + jnp.log(total)


def attend_back(q, qt, go, got, mixed, lse, rows, parts, dq, dkt, dvt, pairs):
    r0, r1 = rows
    low = lanes_low(r1 - r0)
    for pair in range(pairs):
        sl = slice(pair * 128, pair * 128 + 128)
        qp, gp = q[r0:r1, sl], go[r0:r1, sl]
        inner = gp.astype(F32) * mixed[r0:r1, sl].astype(F32)
        halves = []
        for h in range(2):
            hs = slice(pair * 128 + h * 64, pair * 128 + h * 64 + 64)
            qh, gh = head_of(qp, low, h), head_of(gp, low, h)
            delta = jnp.sum(head_of(inner, low, h), axis=1, keepdims=True)
            log_total = lse[r0:r1, hs.start : hs.start + 1]
            dq_h = None
            for s, (k, v, lo, hi, _) in zip(scores_of(qh, parts, sl), parts):
                p = jnp.exp(s - log_total)
                dp = dot(gh, v[lo:hi, sl], NT)
                ds = (p * (dp - delta)).astype(BF)
                dvt[hs, lo:hi] += dot(got[hs, r0:r1], p.astype(BF))
                dkt[hs, lo:hi] += dot(qt[hs, r0:r1], ds)
                term = dot(ds, k[lo:hi, sl])
                dq_h = term if dq_h is None else dq_h + term
            halves.append(dq_h)
        dq[r0:r1, sl] = (jnp.where(low, halves[0], halves[1]) * SCALE).astype(BF)


def gelu_parts(g):
    t = jnp.tanh(GELU_C * (g + GELU_A * g * g * g))
    return 0.5 * g * (1.0 + t), t


def project_rows(ring, start, length, step, gain, wq, wk, wv, xr, q, k, v):
    for r in range(0, length, step):
        x = rotated_rows(ring, wrap(r + start, length), step)
        xr[r : r + step, :] = x.astype(BF)
        n = (x * inverse_rms(x) * gain).astype(BF)
        q[r : r + step, :] = (dot(n, wq[...]).astype(BF) * SCALE).astype(BF)
        k[r : r + step, :] = dot(n, wk[...]).astype(BF)
        v[r : r + step, :] = dot(n, wv[...]).astype(BF)


def put_back(ring, start, length, extra, step, out):
    ring[length : length + extra, :] = ring[0:extra, :]
    for r in range(0, length, step):
        at = r - start
        at = jnp.where(at < 0, at + length, at)
        out[r : r + step, :] = rotated_rows(ring, at, step).astype(out.dtype)


def enc_forward_kernel(
    big, counts, x, qkv, wo, gu, wd, gains, out, memory, xr, q, k, v, mixed, lse, mid, ring, bias
):
    length = x.shape[0]
    rest = length - big
    step = rest
    ends = bounds(counts)
    _, start = big_plot(counts, ends, big)
    gain0 = gains[0:1, :].astype(F32)
    gain1 = gains[1:2, :].astype(F32)
    fill_rotation(ring, x, length, step + 8)
    project_rows(ring, start, length, step, gain0, qkv.at[0], qkv.at[1], qkv.at[2], xr, q, k, v)
    sq = segments(iota((rest, rest), 0) + big, start, ends, length)
    sk = segments(iota((rest, rest), 1) + big, start, ends, length)
    bias[...] = jnp.where(sq == sk, 0.0, NEG)
    pairs = q.shape[1] // 128
    for r in range(0, big, step):
        attend(q, (r, r + step), [(k, v, 0, big, None)], mixed, lse, pairs)
    attend(q, (big, length), [(k, v, big, length, lambda: bias[...])], mixed, lse, pairs)
    for r in range(0, length, step):
        rows = slice(r, r + step)
        m = xr[rows, :].astype(F32) + dot(mixed[rows, :], wo[...])
        mid[rows, :] = m
        n = (m * inverse_rms(m) * gain1).astype(BF)
        act, _ = gelu_parts(dot(n, gu[0]))
        hidden = (act * dot(n, gu[1])).astype(BF)
        total = m + dot(hidden, wd[...])
        ring[rows, :] = total
        memory[rows, :] = total.astype(BF)
    put_back(ring, start, length, step + 8, step, out)


def self_bias(bias, big, start, ends, length):
    shape = (big, big)
    row, col = iota(shape, 0), iota(shape, 1)
    bias[0, :, :] = jnp.where(row >= col, 0.0, NEG)
    same = segments(row + big, start, ends, length) == segments(col + big, start, ends, length)
    bias[1, :, :] = jnp.where(jnp.logical_and(row >= col, same), 0.0, NEG)


def self_tiles(big, bias, k, v):
    half = big // 2
    for b in range(2):
        at = b * big
        for t in range(2):
            lo, hi = t * half, (t + 1) * half
            part = (k, v, at, at + hi, lambda b=b, lo=lo, hi=hi: bias[b, lo:hi, 0:hi])
            yield (at + lo, at + hi), [part]


def cross_setup(ends_d, start_d, big_d, length_d, index_e, start_e, ends_e, big_e, length_e, bias):
    shape = (length_d - big_d, length_e - big_e)
    key = segments(iota(shape, 1) + big_e, start_e, ends_e, length_e)
    for b in range(2):
        query = segments(iota(shape, 0) + b * big_d, start_d, ends_d, length_d)
        bias[b, :, :] = jnp.where(query == key, 0.0, NEG)


def cross_run(same, big_d, length_d, big_e, length_e, rest_col, bias, k, v, run):
    first, second = (0, big_d), (big_d, length_d)
    whole = (k, v, 0, big_e, None)
    masked = (k, v, 0, big_e, rest_col)
    small0 = (k, v, big_e, length_e, lambda: bias[0])
    small1 = (k, v, big_e, length_e, lambda: bias[1])

    @pl.when(same)
    def _():
        run(first, [whole])
        run(second, [small1])

    @pl.when(jnp.logical_not(same))
    def _():
        run(first, [small0])
        run(second, [masked, small1])


def dec_forward_kernel(
    big_e, big_d,
    counts_e, counts_d, x, memory, qkv1, wo1, qkv2, wo2, gains,
    xr, q1, k1, v1, mixed1, lse1, after, q2, k2, v2, mixed2, lse2, second,
    ring, bias1, bias2,
):
    length = x.shape[0]
    length_e = memory.shape[0]
    step = big_d
    ends_d, ends_e = bounds(counts_d), bounds(counts_e)
    index_d, start_d = big_plot(counts_d, ends_d, big_d)
    index_e, start_e = big_plot(counts_e, ends_e, big_e)
    gain0 = gains[0:1, :].astype(F32)
    gain1 = gains[1:2, :].astype(F32)
    for r in range(0, length_e, 512):
        m = memory[r : r + 512, :]
        k2[r : r + 512, :] = dot(m, qkv2[1]).astype(BF)
        v2[r : r + 512, :] = dot(m, qkv2[2]).astype(BF)
    fill_rotation(ring, x, length, step + 8)
    project_rows(ring, start_d, length, step, gain0, qkv1.at[0], qkv1.at[1], qkv1.at[2], xr, q1, k1, v1)
    self_bias(bias1, big_d, start_d, ends_d, length)
    pairs = q1.shape[1] // 128
    for rows, parts in self_tiles(big_d, bias1, k1, v1):
        attend(q1, rows, parts, mixed1, lse1, pairs)
    for r in range(0, length, step):
        rows = slice(r, r + step)
        m = xr[rows, :].astype(F32) + dot(mixed1[rows, :], wo1[...])
        after[rows, :] = m
        n = (m * inverse_rms(m) * gain1).astype(BF)
        q2[rows, :] = (dot(n, qkv2[0]).astype(BF) * SCALE).astype(BF)
    cross_setup(ends_d, start_d, big_d, length, index_e, start_e, ends_e, big_e, length_e, bias2)
    seg_col = segments(iota((length - big_d, 1), 0) + big_d, start_d, ends_d, length)
    col = lambda: jnp.where(seg_col == index_e, 0.0, NEG)

    def run(rows, parts):
        attend(q2, rows, parts, mixed2, lse2, pairs)

    cross_run(index_d == index_e, big_d, length, big_e, length_e, col, bias2, k2, v2, run)
    for r in range(0, length, step):
        rows = slice(r, r + step)
        second[rows, :] = after[rows, :] + dot(mixed2[rows, :], wo2[...])


def ffn_back_rows(x, gain, gu, wd, r, n_buf, rb_buf, h_buf, dg_buf, du_buf, rows):
    n = (x * inverse_rms(x) * gain).astype(BF)
    g, u = dot(n, gu[0]), dot(n, gu[1])
    act, t = gelu_parts(g)
    h = (act * u).astype(BF)
    rb = r.astype(BF)
    gh = dot(rb, wd[...], NT)
    slope = 0.5 * (1.0 + t) + (0.5 * GELU_C) * g * (1.0 - t * t) * (1.0 + (3.0 * GELU_A) * g * g)
    dg = (gh * u * slope).astype(BF)
    du = (gh * act).astype(BF)
    n_buf[rows, :] = n
    rb_buf[rows, :] = rb
    h_buf[rows, :] = h
    dg_buf[rows, :] = dg
    du_buf[rows, :] = du
    return h, dot(dg, gu[0], NT) + dot(du, gu[1], NT)


def ffn_weight_grads(n_buf, rb_buf, h_buf, dg_buf, du_buf, d_gu, d_down):
    d_down[...] = dot(h_buf[...], rb_buf[...], TN)
    d_gu[0, :, :] = dot(n_buf[...], dg_buf[...], TN)
    d_gu[1, :, :] = dot(n_buf[...], du_buf[...], TN)


def row_mask(start, ends, length, r, step):
    slot = wrap(iota((step, 1), 0) + r + start, length)
    return slot < ends[-1]


def dec_ffn_kernel(
    big_d, counts_d, second, cot, gu, wd, gain,
    out, grad_second, d_gu, d_down, d_gain,
    ring, n_buf, rb_buf, h_buf, dg_buf, du_buf,
):
    length = second.shape[0]
    step = big_d
    ends = bounds(counts_d)
    _, start = big_plot(counts_d, ends, big_d)
    gain_row = gain[0:1, :].astype(F32)
    fill_rotation(ring, cot, length, step + 8)
    for r in range(0, length, step):
        rows = slice(r, r + step)
        c = rotated_rows(ring, wrap(r + start, length), step)
        grad_second[rows, :] = jnp.where(row_mask(start, ends, length, r, step), c, 0.0)
    total = None
    for r in range(0, length, step):
        rows = slice(r, r + step)
        x = second[rows, :]
        c = grad_second[rows, :]
        h, gn = ffn_back_rows(x, gain_row, gu, wd, c, n_buf, rb_buf, h_buf, dg_buf, du_buf, rows)
        ring[rows, :] = x + dot(h, wd[...])
        gx, gg = norm_back(x, gain_row, gn)
        grad_second[rows, :] = c + gx
        total = gg if total is None else total + gg
    d_gain[...] = total
    ffn_weight_grads(n_buf, rb_buf, h_buf, dg_buf, du_buf, d_gu, d_down)
    put_back(ring, start, length, step + 8, step, out)


def enc_ffn_kernel(
    big_e, counts_e, mid, cot, grad_memory, gu, wd, gains,
    grad_mid, d_gu, d_down, d_gain,
    ring, n_buf, rb_buf, h_buf, dg_buf, du_buf,
):
    length = mid.shape[0]
    step = length - big_e
    ends = bounds(counts_e)
    _, start = big_plot(counts_e, ends, big_e)
    gain_row = gains[1:2, :].astype(F32)
    fill_rotation(ring, cot, length, step + 8)
    total = None
    for r in range(0, length, step):
        rows = slice(r, r + step)
        c = rotated_rows(ring, wrap(r + start, length), step)
        c = jnp.where(row_mask(start, ends, length, r, step), c, 0.0) + grad_memory[rows, :]
        x = mid[rows, :]
        _, gn = ffn_back_rows(x, gain_row, gu, wd, c, n_buf, rb_buf, h_buf, dg_buf, du_buf, rows)
        gx, gg = norm_back(x, gain_row, gn)
        grad_mid[rows, :] = c + gx
        total = gg if total is None else total + gg
    d_gain[...] = total
    ffn_weight_grads(n_buf, rb_buf, h_buf, dg_buf, du_buf, d_gu, d_down)


def mixed_grads(r, wo, mixed, rb, go, got, d_wo, step):
    for at in range(0, r.shape[0], step):
        rows = slice(at, at + step)
        b = r[rows, :].astype(BF)
        rb[rows, :] = b
        g = dot(b, wo[...], NT).astype(BF)
        go[rows, :] = g
        got[:, rows] = g.T
    d_wo[...] = dot(mixed[...], rb[...], TN)


def cross_back_kernel(
    big_e, big_d,
    counts_e, counts_d, grad_second, after, memory, q, k, v, mixed, lse, qkv, wo, gains,
    grad_first, grad_memory, d_qkv, d_wo, d_gain,
    rb, go, got, qt, dq, dkt, dvt, dk, dv, n_buf, bias,
):
    length, length_e = after.shape[0], memory.shape[0]
    step = big_d
    ends_d, ends_e = bounds(counts_d), bounds(counts_e)
    index_d, start_d = big_plot(counts_d, ends_d, big_d)
    index_e, start_e = big_plot(counts_e, ends_e, big_e)
    gain_row = gains[1:2, :].astype(F32)
    mixed_grads(grad_second, wo, mixed, rb, go, got, d_wo, step)
    for r in range(0, length, step):
        qt[:, r : r + step] = q[r : r + step, :].T
    dkt[...] = jnp.zeros_like(dkt)
    dvt[...] = jnp.zeros_like(dvt)
    cross_setup(ends_d, start_d, big_d, length, index_e, start_e, ends_e, big_e, length_e, bias)
    seg_col = segments(iota((length - big_d, 1), 0) + big_d, start_d, ends_d, length)
    col = lambda: jnp.where(seg_col == index_e, 0.0, NEG)
    pairs = q.shape[1] // 128

    def run(rows, parts):
        attend_back(q, qt, go, got, mixed, lse, rows, parts, dq, dkt, dvt, pairs)

    cross_run(index_d == index_e, big_d, length, big_e, length_e, col, bias, k, v, run)
    for r in range(0, length_e, 512):
        cols = slice(r, r + 512)
        dk[cols, :] = dkt[:, cols].T.astype(BF)
        dv[cols, :] = dvt[:, cols].T.astype(BF)
        grad_memory[cols, :] = dot(dk[cols, :], qkv[1], NT) + dot(dv[cols, :], qkv[2], NT)
    total = None
    for r in range(0, length, step):
        rows = slice(r, r + step)
        x = after[rows, :]
        n_buf[rows, :] = (x * inverse_rms(x) * gain_row).astype(BF)
        gx, gg = norm_back(x, gain_row, dot(dq[rows, :], qkv[0], NT))
        grad_first[rows, :] = grad_second[rows, :] + gx
        total = gg if total is None else total + gg
    d_gain[...] = total
    d_qkv[0, :, :] = dot(n_buf[...], dq[...], TN)
    d_qkv[1, :, :] = dot(memory[...], dk[...], TN)
    d_qkv[2, :, :] = dot(memory[...], dv[...], TN)


def self_back_tail(
    length, step, grad, xr, qkv, gain_row, start, dq, dkt, dvt, dk, dv, n_buf, ring, d_qkv, d_gain, out
):
    total = None
    for r in range(0, length, step):
        rows = slice(r, r + step)
        dk[rows, :] = dkt[:, rows].T.astype(BF)
        dv[rows, :] = dvt[:, rows].T.astype(BF)
        x = xr[rows, :].astype(F32)
        n_buf[rows, :] = (x * inverse_rms(x) * gain_row).astype(BF)
        gn = dot(dq[rows, :], qkv[0], NT) + dot(dk[rows, :], qkv[1], NT) + dot(dv[rows, :], qkv[2], NT)
        gx, gg = norm_back(x, gain_row, gn)
        ring[rows, :] = grad[rows, :] + gx
        total = gg if total is None else total + gg
    d_gain[...] = total
    d_qkv[0, :, :] = dot(n_buf[...], dq[...], TN)
    d_qkv[1, :, :] = dot(n_buf[...], dk[...], TN)
    d_qkv[2, :, :] = dot(n_buf[...], dv[...], TN)
    put_back(ring, start, length, step + 8, step, out)


def dec_self_back_kernel(
    big_d,
    counts_d, grad_first, xr, q, k, v, mixed, lse, qkv, wo, gains,
    out, d_qkv, d_wo, d_gain,
    ring, rb, go, got, qt, dq, dkt, dvt, dk, dv, n_buf, bias,
):
    length = xr.shape[0]
    step = big_d
    ends = bounds(counts_d)
    _, start = big_plot(counts_d, ends, big_d)
    gain_row = gains[0:1, :].astype(F32)
    mixed_grads(grad_first, wo, mixed, rb, go, got, d_wo, step)
    for r in range(0, length, step):
        qt[:, r : r + step] = q[r : r + step, :].T
    dkt[...] = jnp.zeros_like(dkt)
    dvt[...] = jnp.zeros_like(dvt)
    self_bias(bias, big_d, start, ends, length)
    for rows, parts in self_tiles(big_d, bias, k, v):
        attend_back(q, qt, go, got, mixed, lse, rows, parts, dq, dkt, dvt, q.shape[1] // 128)
    self_back_tail(
        length, step, grad_first, xr, qkv, gain_row, start, dq, dkt, dvt, dk, dv, n_buf, ring, d_qkv, d_gain, out
    )


def enc_self_back_kernel(
    big_e,
    counts_e, grad_mid, xr, q, k, v, mixed, lse, qkv, wo, gains,
    out, d_qkv, d_wo, d_gain,
    ring, rb, go, got, qt, dq, dkt, dvt, dk, dv, n_buf, bias,
):
    length = xr.shape[0]
    rest = length - big_e
    step = rest
    ends = bounds(counts_e)
    _, start = big_plot(counts_e, ends, big_e)
    gain_row = gains[0:1, :].astype(F32)
    mixed_grads(grad_mid, wo, mixed, rb, go, got, d_wo, step)
    for r in range(0, length, step):
        qt[:, r : r + step] = q[r : r + step, :].T
    dkt[...] = jnp.zeros_like(dkt)
    dvt[...] = jnp.zeros_like(dvt)
    sq = segments(iota((rest, rest), 0) + big_e, start, ends, length)
    sk = segments(iota((rest, rest), 1) + big_e, start, ends, length)
    bias[...] = jnp.where(sq == sk, 0.0, NEG)
    pairs = q.shape[1] // 128
    for r in range(0, big_e, step):
        attend_back(q, qt, go, got, mixed, lse, (r, r + step), [(k, v, 0, big_e, None)], dq, dkt, dvt, pairs)
    parts = [(k, v, big_e, length, lambda: bias[...])]
    attend_back(q, qt, go, got, mixed, lse, (big_e, length), parts, dq, dkt, dvt, pairs)
    self_back_tail(
        length, step, grad_mid, xr, qkv, gain_row, start, dq, dkt, dvt, dk, dv, n_buf, ring, d_qkv, d_gain, out
    )


def call(kernel, name, scalars, arrays, outs, scratch, flops):
    vmem = pl.BlockSpec(memory_space=pltpu.VMEM)
    smem = pl.BlockSpec(memory_space=pltpu.SMEM)
    size = sum(a.size * a.dtype.itemsize for a in arrays)
    size += sum(o.size * o.dtype.itemsize for o in outs)
    return pl.pallas_call(
        kernel,
        out_shape=tuple(outs),
        in_specs=[smem] * len(scalars) + [vmem] * len(arrays),
        out_specs=tuple([vmem] * len(outs)),
        scratch_shapes=[pltpu.VMEM(s, d) for s, d in scratch],
        compiler_params=pltpu.CompilerParams(vmem_limit_bytes=VMEM_LIMIT),
        cost_estimate=pl.CostEstimate(flops=flops, bytes_accessed=size, transcendentals=0),
        name=name,
    )(*scalars, *arrays)


VMEM_LIMIT = 58 << 20


def like(shape, dtype):
    return jax.ShapeDtypeStruct(shape, dtype)


def one_row(enc_row, dec_row, counts, lengths, enc_w, dec_w, enc_cot, dec_cot):
    enc_qkv, enc_wo, enc_gu, enc_wd, enc_gains = enc_w
    self_qkv, self_wo, cross_qkv, cross_wo, dec_gu, dec_wd, dec_gains, dec_gain = dec_w
    le, width = enc_row.shape
    ld = dec_row.shape[0]
    inner = enc_wo.shape[0]
    ff = enc_wd.shape[0]
    big_e, big_d = le - le // 4, ld // 2
    rest_e = le - big_e

    out_e, memory, xr_e, q_e, k_e, v_e, mixed_e, lse_e, mid = call(
        functools.partial(enc_forward_kernel, big_e), "enc_forward",
        [counts], [enc_row, enc_qkv, enc_wo, enc_gu, enc_wd, enc_gains],
        [like((le, width), BF)] * 3 + [like((le, inner), BF)] * 4 + [like((le, inner), F32), like((le, width), F32)],
        [((le + rest_e + 8, width), F32), ((rest_e, rest_e), F32)], 11_000_000_000,
    )
    xr_d, q1, k1, v1, mixed1, lse1, after, q2, k2, v2, mixed2, lse2, second = call(
        functools.partial(dec_forward_kernel, big_e, big_d), "dec_forward",
        [counts, lengths], [dec_row, memory, self_qkv, self_wo, cross_qkv, cross_wo, dec_gains],
        [like((ld, width), BF)] + [like((ld, inner), BF)] * 4 + [like((ld, inner), F32), like((ld, width), F32)]
        + [like((ld, inner), BF), like((le, inner), BF), like((le, inner), BF), like((ld, inner), BF)]
        + [like((ld, inner), F32), like((ld, width), F32)],
        [((ld + big_d + 8, width), F32), ((2, big_d, big_d), F32), ((2, ld - big_d, rest_e), F32)], 8_000_000_000,
    )

    def ffn_scratch(length, extra):
        return [((length + extra + 8, width), F32), ((length, width), BF), ((length, width), BF)] + [((length, ff), BF)] * 3

    ffn_grads = [like((2, width, ff), F32), like((ff, width), F32), like((1, width), F32)]
    out_d, grad_second, d_dec_gu, d_dec_wd, d_gain3 = call(
        functools.partial(dec_ffn_kernel, big_d), "dec_ffn",
        [lengths], [second, dec_cot, dec_gu, dec_wd, dec_gain.reshape(1, width)],
        [like((ld, width), BF), like((ld, width), F32)] + ffn_grads,
        ffn_scratch(ld, big_d), 10_000_000_000,
    )

    def attn_scratch(lq, lk):
        return [
            ((lq, width), BF), ((lq, inner), BF), ((inner, lq), BF), ((inner, lq), BF), ((lq, inner), BF),
            ((inner, lk), F32), ((inner, lk), F32), ((lk, inner), BF), ((lk, inner), BF), ((lq, width), BF),
        ]

    attn_grads = [like((3, width, inner), F32), like((inner, width), F32), like((1, width), F32)]
    grad_first, grad_memory, d_cross_qkv, d_cross_wo, d_gain2 = call(
        functools.partial(cross_back_kernel, big_e, big_d), "cross_back",
        [counts, lengths], [grad_second, after, memory, q2, k2, v2, mixed2, lse2, cross_qkv, cross_wo, dec_gains],
        [like((ld, width), F32), like((le, width), F32)] + attn_grads,
        attn_scratch(ld, le) + [((2, ld - big_d, rest_e), F32)], 14_000_000_000,
    )
    grad_mid, d_enc_gu, d_enc_wd, d_enc_gain2 = call(
        functools.partial(enc_ffn_kernel, big_e), "enc_ffn",
        [counts], [mid, enc_cot, grad_memory, enc_gu, enc_wd, enc_gains],
        [like((le, width), F32)] + ffn_grads,
        ffn_scratch(le, rest_e), 14_000_000_000,
    )
    grad_dec, d_self_qkv, d_self_wo, d_gain1 = call(
        functools.partial(dec_self_back_kernel, big_d), "dec_self_back",
        [lengths], [grad_first, xr_d, q1, k1, v1, mixed1, lse1, self_qkv, self_wo, dec_gains],
        [like((ld, width), F32)] + attn_grads,
        [((ld + big_d + 8, width), F32)] + attn_scratch(ld, ld) + [((2, big_d, big_d), F32)], 8_000_000_000,
    )
    grad_enc, d_enc_qkv, d_enc_wo, d_enc_gain1 = call(
        functools.partial(enc_self_back_kernel, big_e), "enc_self_back",
        [counts], [grad_mid, xr_e, q_e, k_e, v_e, mixed_e, lse_e, enc_qkv, enc_wo, enc_gains],
        [like((le, width), F32)] + attn_grads,
        [((le + rest_e + 8, width), F32)] + attn_scratch(le, le) + [((rest_e, rest_e), F32)], 18_000_000_000,
    )
    grads = (
        d_enc_qkv, d_enc_wo, d_enc_gu, d_enc_wd, jnp.concatenate([d_enc_gain1, d_enc_gain2]),
        d_self_qkv, d_self_wo, d_cross_qkv, d_cross_wo, d_dec_gu, d_dec_wd,
        jnp.concatenate([d_gain1, d_gain2]), d_gain3.reshape(width),
    )
    return (out_e, out_d, grad_enc, grad_dec), grads


def shards(enc_input, dec_input, patch_counts, table_lengths, *rest):
    enc_w, dec_w, (enc_cot, dec_cot) = rest[:5], rest[5:13], rest[13:]
    outs, totals = [], None
    for b in range(enc_input.shape[0]):
        row, grads = one_row(
            enc_input[b], dec_input[b], patch_counts[b : b + 1], table_lengths[b : b + 1],
            enc_w, dec_w, enc_cot[b], dec_cot[b],
        )
        outs.append(row)
        totals = grads if totals is None else tuple(a + g for a, g in zip(totals, grads))
    placed = tuple(jnp.stack([row[i] for row in outs]) for i in range(4))
    return placed + tuple(lax.psum(totals, AXES))


def solution(mesh):
    rows3 = P(AXES, None, None)
    rows2 = P(AXES, None)
    return jax.shard_map(
        shards,
        mesh=mesh,
        in_specs=(rows3, rows3, rows2, rows2) + (P(),) * 13 + (rows3, rows3),
        out_specs=(rows3,) * 4 + (P(),) * 13,
        check_vma=False,
    )
```

time: 1650 us -> 624 us (0.38)
  matrix products: 491 us -> 0 us
  other arithmetic: 386 us -> 0.01 us
  local copies, waits for them, and re-layouts: 265 us -> 23.7 us
  Pallas kernels: 0 us -> 202 us
  waiting for transfers between devices: 474 us -> 330 us
  blocking collectives: 0 us -> 43.8 us
    dot_general x103 -> x0, matrix products: 491 us -> none  [the longest x7 83.2 us: one_block(): jnp.einsum('qhd,khd->hqk', grad_block, value_heads, preferred_element_typ...]
    unnamed x3 -> x1, waiting for transfers between devices: 359 us -> 0.02 us
    psum x0 -> x1, waiting for transfers between devices: none -> 330 us  [shards(): return placed + tuple(lax.psum(totals, AXES))]
    all_gather x1 -> x0, other arithmetic: 223 us -> none  [shards(): lax.all_gather(all_shares, ('dp', 'batch'), axis=0, tiled=True)]
    pallas_call x0 -> x7, Pallas kernels: none -> 202 us  [call(): pl.pallas_call(kernel, out_shape=tuple(outs), in_specs=[smem] * len(scala...]
    all_gather x1 -> x0, waiting for transfers between devices: 115 us -> none  [shards(): lax.all_gather(all_shares, ('dp', 'batch'), axis=0, tiled=True)]
    convert_element_type x18 -> x0, other arithmetic: 101 us -> none  [the longest x7 96 us: one_block(): grad_scores = (attn_probs * (grad_probs - inner_sum)).astype(jnp.bfloat16)]
    reshape x18 -> x1, local copies, waits for them, and re-layouts: 93.6 us -> 1.26 us  [one_row(): dec_gain.reshape(1, width)]
  transfers between devices with their start and end apart: 2 -> 1, of which waited for: 2 -> 1; matrix products, arithmetic and copies ran while one was open for 1% -> 0% of each run, Pallas kernels for 0% -> 0%
where the time goes in v1:
time: 624 us; the launch traced here: 614 us
  waiting for transfers between devices  330 us (53%)
  Pallas kernels  202 us (32%)
  blocking collectives  43.8 us (7%)
  local copies, waits for them, and re-layouts  23.7 us (4%)
  between operations  14.5 us (2%)
    psum x1, waiting for transfers between devices, shards(): return placed + tuple(lax.psum(totals, AXES))  330 us
    pallas_call x7, Pallas kernels, call(): pl.pallas_call(kernel, out_shape=tuple(outs), in_specs=[smem] * len(scala...  202 us
    psum x1, blocking collectives, shards(): return placed + tuple(lax.psum(totals, AXES))  43.8 us
    unnamed x36, local copies, waits for them, and re-layouts  22.5 us
  transfers between devices with their start and end apart: 1, of which 1 were waited for; matrix products, arithmetic and copies ran while one was open for 0% of the time, Pallas kernels for 0%

profile of v1, /device:TPU:0, one launch (start us, length us, event | category | flops | bytes accessed | tf_op | source)
XLA Modules:
  0.0 614.5 jit_solution(4417652429990199453)
XLA Ops:
  7.2 1.3 reshape.40.gain
  8.5 30.9 %enc_forward.1 = (bf16[1536,512]{1,0:T(8,128)(2,1)}, bf16[1536,512]{1,0:T(8,128)(2,1)}, bf16[1536,512]{1,0:T(8,128)(2,1)}, bf16[1536,384]{1,0:T(8,128)(2,1)}, bf...) custom-call(s32[1,4]{1,0:T(1,128)} %counts_e.7, ...), custom_call_target="tpu_custom_call" | custom-call | flops 11000000512 | bytes 21235712 | tf_op jit(solution)/shard_map/enc_forward/pallas_call | solution.py:526
  39.4 36.1 %dec_forward.1 = (bf16[1024,512]{1,0:T(8,128)(2,1)}, bf16[1024,384]{1,0:T(8,128)(2,1)}, bf16[1024,384]{1,0:T(8,128)(2,1)}, bf16[1024,384]{1,0:T(8,128)(2,1)}, bf...) custom-call(s32[1,4]{1,0:T(1,128)} %counts_e.7, ...), custom_call_target="tpu_custom_call" | custom-call | flops 8000000000 | bytes 21235712 | tf_op jit(solution)/shard_map/dec_forward/pallas_call | solution.py:526
  75.5 17.3 %dec_ffn.1 = (bf16[1024,512]{1,0:T(8,128)(2,1)}, f32[1024,512]{1,0:T(8,128)}, f32[2,512,1024]{2,1,0:T(8,128)}, f32[1024,512]{1,0:T(8,128)}, f32[1,512]{1,0:T(1,128)}) custom-call(s32[1,4]{1,0:T(1,128)} %counts_d.7, f32[1024,512]{1,0:T(8,128)} %get-tuple-element.63.second, bf16[1024,512]{1,0:T(8,128)(2,1)} %bitcast.13, bf16[2,512,1024]{2,1,0:T(8,128)(2,1)} %gu.4, ...), custom_call_target="tpu_custom_call" | custom-call | flops 10000000000 | bytes 15731712 | tf_op jit(solution)/shard_map/dec_ffn/pallas_call | solution.py:526
  92.8 38.4 %cross_back.1 = (f32[1024,512]{1,0:T(8,128)}, f32[1536,512]{1,0:T(8,128)}, f32[3,512,384]{2,1,0:T(8,128)}, f32[384,512]{1,0:T(8,128)}, f32[1,512]{1,0:T(1,128)}) custom-call(s32[1,4]{1,0:T(1,128)} %counts_e.7, s32[1,4]{1,0:T(1,128)} %counts_d.7, f32[1024,512]{1,0:T(8,128)} %get-tuple-element.66.grad_second, f32[1024,512]{1,0:T(8,128)} %get-tuple-element.67.after, ...), custom_call_target="tpu_custom_call" | custom-call | flops 14000000000 | bytes 21237760 | tf_op jit(solution)/shard_map/cross_back/pallas_call | solution.py:526
  131.2 23.3 %enc_ffn.1 = (f32[1536,512]{1,0:T(8,128)}, f32[2,512,1024]{2,1,0:T(8,128)}, f32[1024,512]{1,0:T(8,128)}, f32[1,512]{1,0:T(1,128)}) custom-call(s32[1,4]{1,0:T(1,128)} %counts_e.7, f32[1536,512]{1,0:T(8,128)} %get-tuple-element.65.mid, bf16[1536,512]{1,0:T(8,128)(2,1)} %bitcast.11, f32[1536,512]{1,0:T(8,128)} %get-tuple-element.73.grad_memory, ...), custom_call_target="tpu_custom_call" | custom-call | flops 14000000000 | bytes 20451328 | tf_op jit(solution)/shard_map/enc_ffn/pallas_call | solution.py:526
  154.5 18.4 %dec_self_back.1 = (f32[1024,512]{1,0:T(8,128)}, f32[3,512,384]{2,1,0:T(8,128)}, f32[384,512]{1,0:T(8,128)}, f32[1,512]{1,0:T(1,128)}) custom-call(s32[1,4]{1,0:T(1,128)} %counts_d.7, f32[1024,512]{1,0:T(8,128)} %get-tuple-element.82.grad_first, bf16[1024,512]{1,0:T(8,128)(2,1)} %get-tuple-element.83.xr, bf16[1024,384]{1,0:T(8,128)(2,1)} %get-tuple-element.84.q, ...), custom_call_target="tpu_custom_call" | custom-call | flops 8000000000 | bytes 14684160 | tf_op jit(solution)/shard_map/dec_self_back/pallas_call | solution.py:526
  172.9 37.5 %enc_self_back.1 = (f32[1536,512]{1,0:T(8,128)}, f32[3,512,384]{2,1,0:T(8,128)}, f32[384,512]{1,0:T(8,128)}, f32[1,512]{1,0:T(1,128)}) custom-call(s32[1,4]{1,0:T(1,128)} %counts_e.7, f32[1536,512]{1,0:T(8,128)} %get-tuple-element.74.grad_mid, bf16[1536,512]{1,0:T(8,128)(2,1)} %get-tuple-element.75.xr, bf16[1536,384]{1,0:T(8,128)(2,1)} %get-tuple-element.76.q, ...), custom_call_target="tpu_custom_call" | custom-call | flops 17999998976 | bytes 19664896 | tf_op jit(solution)/shard_map/enc_self_back/pallas_call | solution.py:526
  211.2 43.8 %all-reduce = (f32[2,512]{1,0:T(2,128)}, f32[2,512]{1,0:T(2,128)}, f32[512]{0:T(512)}) all-reduce(f32[2,512]{1,0:T(2,128)S(1)} %get-tuple-element.118, f32[2,512]{1,0:T(2,128)S(1)} %get-tuple-element.119, f32[512]{0:T(512)S(1)} %bitcast.9), channel_id=1, replica_groups=mesh['dp'=16,'batch'=2] {'dp','batch'}, use_global_device_ids=true, to_apply=%region_4.0 | all-reduce | flops 2560 | bytes 20480 | tf_op jit(solution)/shard_map/psum | solution.py:631
  255.0 330.4 %all-reduce.4.cloned.1.call-done = (f32[3,512,384]{2,1,0:T(8,128)}, f32[384,512]{1,0:T(8,128)}, f32[2,512,1024]{2,1,0:T(8,128)}, f32[1024,512]{1,0:T(8,128)}, f3...) async-done(((f32[3,512,384]{2,1,0:T(8,128)}, ...) | async-done | bytes 22020112 | tf_op jit(solution)/shard_map/psum | solution.py:631
  585.5 3.4 copy.46
  588.8 2.1 copy.47
  590.9 2.1 copy.48
  593.0 1.0 copy-done.5
  594.0 1.3 copy.49
  595.3 1.1 copy-done.3
  596.4 1.4 copy.50
  598.1 0.9 copy.51
  599.5 1.4 copy.52
  600.9 0.9 copy.53
  601.7 1.1 copy-done
  602.8 2.1 copy.54
  605.0 1.0 copy-done.4
  605.9 1.3 copy.55
  (25 shorter events, 1.5 us)
Async XLA Ops:
  7.2 578.3 %all-reduce.4.cloned.1.call-start = ((), (), s32[]{:S(2)}) async-start(), calls=%async_computation | async-start | bytes 44040192 | tf_op jit(solution)/shard_map/psum | solution.py:631
  210.5 0.7 copy-start.9
  210.5 0.7 copy-start.10
  210.5 0.7 copy-start.11
  210.5 0.7 copy-start.12
  210.5 0.7 copy-start.8
  585.5 5.4 copy-start.1
  590.9 3.1 copy-start.5
  594.0 2.4 copy-start.3
  596.4 1.7 copy-start.7
  596.4 3.0 copy-start.2
  598.1 2.8 copy-start.6
  599.5 3.4 copy-start
  602.8 3.1 copy-start.4
Sparse Core Ops, SparseCore 0:
  210.6 374.7 all-reduce.3
